TPU v7x, 512 devices: a whole 4x4x16 slice. The times are simulated.
512 devices in a mesh: expert: 64 (over z_hi, x, y), dp: 8 (over z_lo, core).
Axes of the slice: x: 4, y: 4, z: 16 (z_hi: 4, z_lo: 4; z = z_hi * 4 + z_lo), core: 2. Of those that a mesh axis runs over, the one named last changes fastest.
Arguments:
- hidden: bfloat16 [65536, 1, 1024], P(('expert', 'dp')), may hold values from -6 to 6
- probs: float32 [65536, 1], P(('expert', 'dp')), may hold values from 0.05 to 1
- expert_ids: int32 [65536, 1], P(('expert', 'dp')), may hold values from 0 to 63; in each aligned block of 128 rows (0 to 127, 128 to 255, ...) at most 4 rows name the same one
- swap_plan: int32 [64], replicated, may hold values from 0 to 1, as said below
- down_weight: bfloat16 [64, 1024, 4096], P('expert', None, 'dp'), may hold values from -0.1875 to 0.1875
- out_grad: bfloat16 [65536, 4096], P(('expert', 'dp')), may hold values from -0.29882812 to 0.29882812
Outputs:
- mixed: bfloat16 [65536, 4096], P(('expert', 'dp'))
- hidden_grad: bfloat16 [65536, 1, 1024], P(('expert', 'dp'))
- prob_grad: float32 [65536, 1], P(('expert', 'dp'))
- weight_grad: bfloat16 [64, 1024, 4096], P('expert', None, 'dp')
Inputs may be any that keep to these rules, and one draw needn't show every extreme that they name: `expert_ids`: each device's 128 tokens name one expert at most 4 times. swap_plan[e] equals swap_plan[e + 32] for e below 32.
All inputs are finite; a program needn't handle non-finite values.
Results may differ from a plain program's by a relative error of at most 0.017.
Values may be sent and summed in bfloat16 or wider, within the bound.
A program may use at most 64 MiB of HBM per device.

v0:
```python
import jax
import jax.numpy as jnp
from jax import lax
from jax.sharding import PartitionSpec as P


def partner(value, axis, apart):
    return lax.ppermute(value, axis, [(i, i ^ 1 << apart) for i in range(lax.axis_size(axis))])


def placing_matrix(route, capacity, experts):
    flat = route.reshape(-1)
    numbers = jnp.arange(experts, dtype=jnp.int32)
    marks = (flat[:, None] == numbers[None, :]).astype(jnp.int32)
    before = jnp.cumsum(marks, axis=0) - marks
    rank = jnp.sum(before * marks, axis=1)
    position = flat * capacity + rank
    slots = jnp.arange(experts * capacity, dtype=jnp.int32)
    return (slots[:, None] == position[None, :]).astype(jnp.bfloat16)


def shards(hidden, probs, expert_ids, swap_plan, down_weight, out_grad):
    experts = lax.axis_size("expert")
    groups = lax.axis_size("dp")
    half_bit = experts.bit_length() - 2
    half = experts // 2
    tok_rows, top, width_ff = hidden.shape
    width = out_grad.shape[1]
    capacity = max(2, 2 * ((tok_rows * top + experts - 1) // experts))
    numbers = jnp.arange(experts, dtype=jnp.int32)
    owner = jnp.where(swap_plan == 1, (numbers + half) % experts, numbers)
    mine = lax.axis_index("expert")
    own_flag = jnp.sum(jnp.where(numbers == mine, swap_plan, 0))
    weights = down_weight[0]
    cols = weights.shape[1]
    moved = partner(down_weight, "expert", half_bit)
    weights = jnp.where(own_flag == 1, moved[0], weights)
    route = jnp.sum(
        jnp.where(expert_ids[:, :, None] == numbers[None, None, :], owner[None, None, :], 0), axis=2
    )
    placing = placing_matrix(route, capacity, experts)
    slot_count = tok_rows * top
    send = jnp.dot(
        placing, hidden.reshape(slot_count, width_ff), preferred_element_type=jnp.float32
    )
    send = send.astype(jnp.bfloat16).reshape(experts, capacity, width_ff)
    arrived = lax.all_to_all(send, "expert", split_axis=0, concat_axis=0, tiled=True)
    rows_all = lax.all_gather(
        arrived.reshape(experts * capacity, width_ff), "dp", axis=0, tiled=True
    )
    local_out = jnp.dot(rows_all, weights, preferred_element_type=jnp.float32).astype(jnp.bfloat16)
    regrouped = lax.all_to_all(
        local_out.reshape(groups, experts * capacity, cols),
        "dp",
        split_axis=0,
        concat_axis=2,
        tiled=True,
    )
    returned = lax.all_to_all(
        regrouped.reshape(experts, capacity, groups * cols),
        "expert",
        split_axis=0,
        concat_axis=0,
        tiled=True,
    )
    slot_out = jnp.dot(
        placing.T, returned.reshape(experts * capacity, width), preferred_element_type=jnp.float32
    )
    slot_wide = slot_out.astype(jnp.bfloat16).astype(jnp.float32).reshape(tok_rows, top, width)
    upstream = out_grad.astype(jnp.float32)
    mixed = jnp.sum(probs[:, :, None] * slot_wide, axis=1).astype(jnp.bfloat16)
    prob_grad = jnp.sum(upstream[:, None, :] * slot_wide, axis=2)
    grad_rows = (
        (probs[:, :, None] * upstream[:, None, :]).astype(jnp.bfloat16).reshape(slot_count, width)
    )
    grad_send = jnp.dot(placing, grad_rows, preferred_element_type=jnp.float32).astype(jnp.bfloat16)
    grad_send = grad_send.reshape(experts, capacity, groups, cols)
    grad_all = lax.all_to_all(
        lax.all_to_all(grad_send, "expert", split_axis=0, concat_axis=0, tiled=True),
        "dp",
        split_axis=2,
        concat_axis=0,
        tiled=True,
    )
    grad_all = grad_all.reshape(groups * experts * capacity, cols)
    summed = lax.psum_scatter(
        lax.dot_general(
            grad_all, weights, (((1,), (1,)), ((), ())), preferred_element_type=jnp.float32
        ).astype(jnp.bfloat16),
        "dp",
        scatter_dimension=0,
        tiled=True,
    )
    grad_buf = summed.reshape(experts, capacity, width_ff)
    hidden_back = lax.all_to_all(grad_buf, "expert", split_axis=0, concat_axis=0, tiled=True)
    hidden_grad = jnp.dot(
        placing.T,
        hidden_back.reshape(experts * capacity, width_ff),
        preferred_element_type=jnp.float32,
    )
    hidden_grad = hidden_grad.astype(jnp.bfloat16).reshape(tok_rows, top, width_ff)
    weight_grad = lax.dot_general(
        rows_all, grad_all, (((0,), (0,)), ((), ())), preferred_element_type=jnp.float32
    ).astype(jnp.bfloat16)
    return (mixed, hidden_grad, prob_grad, weight_grad[None])


def solution(mesh):
    in_specs = (
        P(("expert", "dp"), None, None),
        P(("expert", "dp"), None),
        P(("expert", "dp"), None),
        P(),
        P("expert", None, "dp"),
        P(("expert", "dp"), None),
    )
    out_specs = (
        P(("expert", "dp"), None),
        P(("expert", "dp"), None, None),
        P(("expert", "dp"), None),
        P("expert", None, "dp"),
    )
    return jax.shard_map(shards, mesh=mesh, in_specs=in_specs, out_specs=out_specs, check_vma=False)
```

profile of v0, /device:TPU:25, one launch (start us, length us, event | category | flops | bytes accessed | tf_op | source)
XLA Modules:
  0.0 568.8 jit_solution(1822794470903413676)
XLA Ops:
  7.2 0.0 copy-start
  7.2 0.0 copy-start.2
  7.2 0.0 copy-start.4
  7.2 1.4 fusion.15
  8.6 0.7 select_reduce_fusion.1
  9.3 0.1 fusion.14
  9.4 0.2 reduce_window_sum.11
  9.6 0.2 select_reduce_fusion
  9.8 0.3 convolution_convert_fusion.5
  10.1 1.0 reshape.132
  11.1 20.4 %all-to-all-start = ((bf16[64,4,1024]{2,1,0:T(4,128)(2,1)}), bf16[64,4,1024]{2,1,0:T(4,128)(2,1)S(1)}, u32[]{:S(2)}, u32[]{:S(2)}) async-start(bf16[64,4,1024]{2,1,0:T(4,128)(2,1)} %reshape.132), calls=%async_computation | async-start | bytes 1048576 | tf_op jit(solution)/shard_map/all_to_all | solution.py:47
  31.5 0.0 copy-done.2
  31.5 0.0 copy-done.4
  31.5 0.8 convolution_convert_fusion
  32.3 0.9 copy.21
  33.2 2.4 copy.19
  35.6 22.7 %all-to-all-done = bf16[64,4,1024]{2,1,0:T(4,128)(2,1)S(1)} async-done(((bf16[64,4,1024]{2,1,0:T(4,128)(2,1)}), bf16[64,4,1024]{2,1,0:T(4,128)(2,1)S(1)}, u32[]{:S(2)}, u32[]{:S(2)}) %all-to-all-start) | async-done | bytes 524320 | tf_op jit(solution)/shard_map/all_to_all | solution.py:47
  58.3 0.8 copy-done.3
  59.1 12.4 %all-to-all-start.3 = ((bf16[64,4,8,512]{3,1,2,0:T(4,128)(2,1)}), bf16[64,4,8,512]{3,1,2,0:T(4,128)(2,1)S(1)}, u32[]{:S(2)}, u32[]{:S(2)}) async-start(bf16[64,4,8,512]{3,1,2,0:T(4,128)(2,1)} %copy.19), calls=%async_computation.3 | async-start | bytes 4194304 | tf_op jit(solution)/shard_map/all_to_all | solution.py:79
  71.6 0.0 all-gather.2.cloned.1.call-start
  71.6 2.0 reshape.133
  73.6 0.0 all-gather.2.cloned.1.call-update
  73.6 76.5 %all-to-all-done.3 = bf16[64,4,8,512]{3,1,2,0:T(4,128)(2,1)S(1)} async-done(((bf16[64,4,8,512]{3,1,2,0:T(4,128)(2,1)}), bf16[64,4,8,512]{3,1,2,0:T(4,128)(2,1)S(1)}, u32[]{:S(2)}, u32[]{:S(2)}) %all-to-all-start.3) | async-done | bytes 2097184 | tf_op jit(solution)/shard_map/all_to_all | solution.py:79
  150.0 2.1 copy.20
  152.2 47.5 %all-to-all-start.4 = ((bf16[64,4,8,512]{3,1,0,2:T(4,128)(2,1)}), bf16[64,4,8,512]{3,1,0,2:T(4,128)(2,1)S(1)}, u32[]{:S(2)}, u32[]{:S(2)}) async-start(bf16[64,4,8,512]{3,1,0,2:T(4,128)(2,1)} %copy.20), calls=%async_computation.4 | async-start | bytes 4194304 | tf_op jit(solution)/shard_map/all_to_all | solution.py:78
  199.7 6.1 %collective-permute-start = (bf16[1,1024,512]{2,1,0:T(8,128)(2,1)}, bf16[1,1024,512]{2,1,0:T(8,128)(2,1)}, u32[]{:S(2)}, u32[]{:S(2)}) collective-permute-start(bf16[1,1024,512]{2,1,0:T(8,128)(2,1)} %param.10), channel_id=1, source_target_pairs={{0,256},{8,264},{16,272},{24,280},{32,288},{40,296},{48,304},{56,3... | collective-permute-start | bytes 3145736 | tf_op jit(solution)/shard_map/ppermute | solution.py:8
  206.5 125.6 %collective-permute-done = bf16[1,1024,512]{2,1,0:T(8,128)(2,1)} collective-permute-done((bf16[1,1024,512]{2,1,0:T(8,128)(2,1)}, bf16[1,1024,512]{2,1,0:T(8,128)(2,1)}, u32[]{:S(2)}, u32[]{:S(2)}) %collective-permute-start) | collective-permute-done | bytes 1048608 | tf_op jit(solution)/shard_map/ppermute | solution.py:8
  332.1 6.2 %convolution_convert_fusion.3 = bf16[2048,512]{1,0:T(8,128)(2,1)} fusion(bf16[2048,1024]{1,0:T(8,128)(2,1)} %all-gather.2.cloned.1.call-done, bf16[1,1024,512]{2,1,0:T(8,128)(2,1)} %collective-permute-done, bf16[1,1024,512]{2,1,0:T(8,128)(2,1)} %param.10, pred[]{:T(512)S(6)} %eq.77), kind=kOutput, calls=%fused_computation.4 | convolution fusion | flops 2149056512 | bytes 8388609 | tf_op jit(solution)/shard_map/dot_general | solution.py:51
  338.3 0.0 all-to-all-done.4
  338.3 6.5 %all-to-all-start.1 = ((bf16[8,256,512]{2,1,0:T(8,128)(2,1)}), bf16[8,256,512]{2,1,0:T(8,128)(2,1)}, u32[]{:S(2)}, u32[]{:S(2)}) async-start(bf16[8,256,512]{2,1,0:T(8,128)(2,1)} %bitcast.38), calls=%async_computation.1 | async-start | bytes 4194304 | tf_op jit(solution)/shard_map/all_to_all | solution.py:52
  344.8 0.0 reduce-scatter.2.cloned.1.call-start
  344.8 2.1 reshape.138
  346.9 6.2 %convolution_convert_fusion.2 = bf16[2048,1024]{1,0:T(8,128)(2,1)} fusion(bf16[2048,512]{1,0:T(8,128)(2,1)} %reshape.138, bf16[1,1024,512]{2,1,0:T(8,128)(2,1)} %collective-permute-done, bf16[1,1024,512]{2,1,0:T(8,128)(2,1)} %param.10, pred[]{:T(512)S(6)} %eq.77), kind=kOutput, calls=%fused_computation.3 | convolution fusion | flops 2150105088 | bytes 8388609 | tf_op jit(solution)/shard_map/dot_general | solution.py:87
  353.1 0.0 reduce-scatter.2.cloned.1.call-update
  353.1 59.0 %all-to-all-done.1 = bf16[8,256,512]{2,1,0:T(8,128)(2,1)} async-done(((bf16[8,256,512]{2,1,0:T(8,128)(2,1)}), bf16[8,256,512]{2,1,0:T(8,128)(2,1)}, u32[]{:S(2)}, u32[]{:S(2)}) %all-to-all-start.1) | async-done | bytes 2097184 | tf_op jit(solution)/shard_map/all_to_all | solution.py:52
  412.1 2.8 copy.18
  414.9 2.8 reshape.135
  417.7 13.8 %all-to-all-start.2 = ((bf16[64,4,4096]{2,1,0:T(4,128)(2,1)}), bf16[64,4,4096]{2,1,0:T(4,128)(2,1)S(1)}, u32[]{:S(2)}, u32[]{:S(2)}) async-start(bf16[64,4,4096]{2,1,0:T(4,128)(2,1)} %reshape.135), calls=%async_computation.2 | async-start | bytes 4194304 | tf_op jit(solution)/shard_map/all_to_all | solution.py:59
  431.5 0.4 reduce-scatter.2.cloned.1.call-done
  431.8 2.0 reshape.139
  433.9 94.0 %all-to-all-done.2 = bf16[64,4,4096]{2,1,0:T(4,128)(2,1)S(1)} async-done(((bf16[64,4,4096]{2,1,0:T(4,128)(2,1)}), bf16[64,4,4096]{2,1,0:T(4,128)(2,1)S(1)}, u32[]{:S(2)}, u32[]{:S(2)}) %all-to-all-start.2) | async-done | bytes 2097184 | tf_op jit(solution)/shard_map/all_to_all | solution.py:59
  527.9 11.7 %all-to-all-start.5 = ((bf16[64,4,1024]{2,1,0:T(4,128)(2,1)}), bf16[64,4,1024]{2,1,0:T(4,128)(2,1)}, u32[]{:S(2)}, u32[]{:S(2)}) async-start(bf16[64,4,1024]{2,1,0:T(4,128)(2,1)} %reshape.139), calls=%async_computation.6 | async-start | bytes 1048576 | tf_op jit(solution)/shard_map/all_to_all | solution.py:95
  539.6 6.2 %fusion.3 = bf16[1,1024,512]{2,1,0:T(8,128)(2,1)} fusion(bf16[2048,1024]{1,0:T(8,128)(2,1)} %all-gather.2.cloned.1.call-done, bf16[2048,512]{1,0:T(8,128)(2,1)} %reshape.138), kind=kOutput, calls=%fused_computation.11 | convolution fusion | flops 2148007936 | bytes 7340032 | tf_op jit(solution)/shard_map/dot_general | solution.py:102
  545.8 2.5 reshape.136
  548.4 2.2 fusion.2
  550.6 9.3 %all-to-all-done.5 = bf16[64,4,1024]{2,1,0:T(4,128)(2,1)} async-done(((bf16[64,4,1024]{2,1,0:T(4,128)(2,1)}), bf16[64,4,1024]{2,1,0:T(4,128)(2,1)}, u32[]{:S(2)}, u32[]{:S(2)}) %all-to-all-start.5) | async-done | bytes 524320 | tf_op jit(solution)/shard_map/all_to_all | solution.py:95
  559.9 1.2 reshape.140
  561.0 1.0 fusion.4
  (6 shorter events, 0.0 us)
Async XLA Ops:
  7.2 2.6 copy-start
  7.2 24.3 %copy-start.2 = (bf16[128,4096]{1,0:T(8,128)(2,1)S(1)}, bf16[128,4096]{1,0:T(8,128)(2,1)}, u32[]{:S(2)}) copy-start(bf16[128,4096]{1,0:T(8,128)(2,1)} %param.11) | copy-start | bytes 3145732
  7.2 24.3 %copy-start.4 = (f32[128,1]{0,1:T(1,128)S(1)}, f32[128,1]{0,1:T(1,128)}, u32[]{:S(2)}) copy-start(f32[128,1]{0,1:T(1,128)} %param.7) | copy-start | bytes 1540
  11.1 47.2 %all-to-all-start = ((bf16[64,4,1024]{2,1,0:T(4,128)(2,1)}), bf16[64,4,1024]{2,1,0:T(4,128)(2,1)S(1)}, u32[]{:S(2)}, u32[]{:S(2)}) async-start(bf16[64,4,1024]{2,1,0:T(4,128)(2,1)} %reshape.132), calls=%async_computation | async-start | bytes 1048576 | tf_op jit(solution)/shard_map/all_to_all | solution.py:47
  58.3 0.8 copy-start.3
  59.1 90.9 %all-to-all-start.3 = ((bf16[64,4,8,512]{3,1,2,0:T(4,128)(2,1)}), bf16[64,4,8,512]{3,1,2,0:T(4,128)(2,1)S(1)}, u32[]{:S(2)}, u32[]{:S(2)}) async-start(bf16[64,4,8,512]{3,1,2,0:T(4,128)(2,1)} %copy.19), calls=%async_computation.3 | async-start | bytes 4194304 | tf_op jit(solution)/shard_map/all_to_all | solution.py:79
  71.6 260.5 %all-gather.2.cloned.1.call-start = ((), (), s32[]{:S(2)}) async-start(), calls=%async_computation.7 | async-start | bytes 4718592 | tf_op jit(solution)/shard_map/all_gather | solution.py:48
  152.2 186.1 %all-to-all-start.4 = ((bf16[64,4,8,512]{3,1,0,2:T(4,128)(2,1)}), bf16[64,4,8,512]{3,1,0,2:T(4,128)(2,1)S(1)}, u32[]{:S(2)}, u32[]{:S(2)}) async-start(bf16[64,4,8,512]{3,1,0,2:T(4,128)(2,1)} %copy.20), calls=%async_computation.4 | async-start | bytes 4194304 | tf_op jit(solution)/shard_map/all_to_all | solution.py:78
  199.7 132.4 %collective-permute-start = (bf16[1,1024,512]{2,1,0:T(8,128)(2,1)}, bf16[1,1024,512]{2,1,0:T(8,128)(2,1)}, u32[]{:S(2)}, u32[]{:S(2)}) collective-permute-start(bf16[1,1024,512]{2,1,0:T(8,128)(2,1)} %param.10), channel_id=1, source_target_pairs={{0,256},{8,264},{16,272},{24,280},{32,288},{40,296},{48,304},{56,3... | collective-permute-start | bytes 3145736 | tf_op jit(solution)/shard_map/ppermute | solution.py:8
  338.3 73.8 %all-to-all-start.1 = ((bf16[8,256,512]{2,1,0:T(8,128)(2,1)}), bf16[8,256,512]{2,1,0:T(8,128)(2,1)}, u32[]{:S(2)}, u32[]{:S(2)}) async-start(bf16[8,256,512]{2,1,0:T(8,128)(2,1)} %bitcast.38), calls=%async_computation.1 | async-start | bytes 4194304 | tf_op jit(solution)/shard_map/all_to_all | solution.py:52
  344.8 87.1 %reduce-scatter.2.cloned.1.call-start = ((), (), s32[]{:S(2)}) async-start(), calls=%async_computation.8 | async-start | bytes 4718592 | tf_op jit(solution)/shard_map/reduce_scatter | solution.py:86
  417.7 110.2 %all-to-all-start.2 = ((bf16[64,4,4096]{2,1,0:T(4,128)(2,1)}), bf16[64,4,4096]{2,1,0:T(4,128)(2,1)S(1)}, u32[]{:S(2)}, u32[]{:S(2)}) async-start(bf16[64,4,4096]{2,1,0:T(4,128)(2,1)} %reshape.135), calls=%async_computation.2 | async-start | bytes 4194304 | tf_op jit(solution)/shard_map/all_to_all | solution.py:59
  527.9 11.7 %copy-start.1 = (bf16[64,4,4096]{2,1,0:T(4,128)(2,1)}, bf16[64,4,4096]{2,1,0:T(4,128)(2,1)S(1)}, u32[]{:S(2)}) copy-start(bf16[64,4,4096]{2,1,0:T(4,128)(2,1)S(1)} %all-to-all-done.2) | copy-start | bytes 6291460
  527.9 32.0 %all-to-all-start.5 = ((bf16[64,4,1024]{2,1,0:T(4,128)(2,1)}), bf16[64,4,1024]{2,1,0:T(4,128)(2,1)}, u32[]{:S(2)}, u32[]{:S(2)}) async-start(bf16[64,4,1024]{2,1,0:T(4,128)(2,1)} %reshape.139), calls=%async_computation.6 | async-start | bytes 1048576 | tf_op jit(solution)/shard_map/all_to_all | solution.py:95
Sparse Core Ops, SparseCore 0:
  75.0 130.0 all-gather.1
  353.2 78.5 reduce-scatter.1
where the time goes:
time: 580 us; the launch traced here: 569 us
  waiting for transfers between devices  387 us (67%)
  starting transfers between devices  118 us (20%)
  matrix products  22.9 us (4%)
  local copies, waits for them, and re-layouts  22.6 us (4%)
  between operations  14.8 us (3%)
    ppermute x1, waiting for transfers between devices, partner(): lax.ppermute(value, axis, [(i, i ^ 1 << apart) for i in range(lax.axis_si...  126 us
    all_to_all x1, waiting for transfers between devices, shards(): lax.all_to_all(regrouped.reshape(experts, capacity, groups * cols), 'expe...  94 us
    all_to_all x1, waiting for transfers between devices, shards(): lax.all_to_all(grad_send, 'expert', split_axis=0, concat_axis=0, tiled=True)  76.5 us
    all_to_all x1, waiting for transfers between devices, shards(): lax.all_to_all(local_out.reshape(groups, experts * capacity, cols), 'dp',...  59 us
    all_to_all x1, starting transfers between devices, shards(): lax.all_to_all(lax.all_to_all(grad_send, 'expert', split_axis=0, concat_a...  47.5 us
    all_to_all x1, waiting for transfers between devices, shards(): lax.all_to_all(send, 'expert', split_axis=0, concat_axis=0, tiled=True)  22.7 us
    all_to_all x1, starting transfers between devices, shards(): lax.all_to_all(send, 'expert', split_axis=0, concat_axis=0, tiled=True)  20.4 us
    all_to_all x1, starting transfers between devices, shards(): lax.all_to_all(regrouped.reshape(experts, capacity, groups * cols), 'expe...  13.8 us
  transfers between devices with their start and end apart: 9, of which 7 were waited for; matrix products, arithmetic and copies ran while one was open for 7% of the time, Pallas kernels for 0%

commit v1 on v0

v1 whole, which is shorter than its diff:
```python
import functools

import jax
import jax.numpy as jnp
from jax import lax
from jax.experimental import pallas as pl
from jax.experimental.pallas import tpu as pltpu
from jax.sharding import PartitionSpec as P

MESH = pl.DeviceIdType.MESH
RUNS = 4
CAP = 4
BF16, F32 = jnp.bfloat16, jnp.float32


def dot(a, b, dims):
    return lax.dot_general(a, b, (dims, ((), ())), preferred_element_type=F32)


def done(view, sem):
    pltpu.make_async_copy(view, view, sem).wait()


def kernel(
    sizes, hid, og, probs, codes, flag, w, mixed, hgrad, pgrad, wgrad,
    hs, gs, hz, gz, cz, hx, gx, hr, hr2, gr, place, w2, ox, ot, ou, oz,
    ps, pk, pr, px, pt, pu, pz, dsend, dkeep, drecv,
    z_send, z_recv, x_send, x_recv, b_send, b_recv, p_send, p_recv,
):
    xys, low, tok = sizes
    chips = RUNS * low
    near = 2 * low
    half = hid.shape[1] // 2
    cols = w.shape[1]
    quads = near // 2
    e, d = lax.axis_index("expert"), lax.axis_index("dp")
    zh, xy, zl, c = e // xys, e % xys, d // 2, d % 2
    z = zh * low + zl
    other = 1 - c

    def at_chip(step, core):
        to = (z + step + chips) % chips
        return (to // low) * xys + xy, (to % low) * 2 + core

    far = low * (1 - 2 * c)
    partner = ((zh + RUNS // 2) % RUNS * xys + xy, d)
    sibling = (e, zl * 2 + other)

    def in_plane(n):
        to = (xy + n) % xys
        return to, (zh * xys + to, d)

    def remote(src, dst, ssem, rsem, to):
        return pltpu.make_async_remote_copy(
            src_ref=src, dst_ref=dst, send_sem=ssem, recv_sem=rsem, device_id=to, device_id_type=MESH
        )

    barrier = pltpu.get_barrier_semaphore()

    def greet(to):
        pl.semaphore_signal(barrier, inc=1, device_id=to, device_id_type=MESH)

    def step_of(i):
        return jnp.where(i < low - 1, i - (low - 1), i - (low - 2))

    def hello_z(i, _):
        for core in range(2):
            greet(at_chip(step_of(i), core))
        return 0

    def hello_xy(n, _):
        greet(in_plane(n)[1])
        return 0

    lax.fori_loop(0, near - 2, hello_z, 0)
    for core in range(2):
        greet(at_chip(low, core))
        greet(at_chip(-low, core))
    greet(sibling)
    greet(partner)
    lax.fori_loop(1, xys, hello_xy, 0)
    pl.semaphore_wait(barrier, 2 * (near - 2) + 4 + 2 + xys - 1)

    def z_out(src_of, dst, k):
        def one(step, slot, core):
            remote(src_of(step, core), dst.at[slot * 2 + c], z_send.at[k], z_recv.at[k], at_chip(step, core)).start()

        def go(i, _):
            step = step_of(i)
            for core in range(2):
                one(step, low - 1 - step, core)
            return 0

        lax.fori_loop(0, near - 2, go, 0)
        for core in range(2):
            one(far, near - 1, core)
        mine = (low - 1) * 2 + c
        remote(src_of(0, other), dst.at[mine], z_send.at[k], z_recv.at[k], sibling).start()
        pltpu.make_async_copy(src_of(0, c), dst.at[mine], z_recv.at[k]).start()

    def z_back(src, dst, k):
        def one(step, slot, core, to):
            remote(src.at[slot * 2 + core], dst.at[(low - 1 - step) * 2 + c], z_send.at[k], z_recv.at[k], to).start()

        def go(i, _):
            step = step_of(i)
            for core in range(2):
                one(step, step + low - 1, core, at_chip(step, core))
            return 0

        lax.fori_loop(0, near - 2, go, 0)
        for core in range(2):
            remote(
                src.at[(near - 1) * 2 + core], dst.at[(near - 1) * 2 + c], z_send.at[k], z_recv.at[k],
                at_chip(low * (2 * core - 1), core),
            ).start()
        one(0, low - 1, other, sibling)
        pltpu.make_async_copy(src.at[(low - 1) * 2 + c], dst.at[(low - 1) * 2 + c], z_recv.at[k]).start()

    def x_out(src, dst, k):
        def go(n, _):
            to, dev = in_plane(n)
            remote(src.at[to], dst.at[xy], x_send.at[k], x_recv.at[k], dev).start()
            return 0

        lax.fori_loop(1, xys, go, 0)
        pltpu.make_async_copy(src.at[xy], dst.at[xy], x_recv.at[k]).start()

    z_out(lambda step, core: codes, cz, 0)
    for h in range(2):
        hs[h] = hid[:, h * half : (h + 1) * half]
    z_out(lambda step, core: hs.at[core], hz, 1)
    for g in range(gs.shape[0]):
        up = og[:, g * cols : (g + 1) * cols].astype(F32)
        gs[g] = (probs[...] * up).astype(BF16)
    z_out(lambda step, core: gs.at[((zl + step + low) % low) * 2 + core], gz, 2)

    done(cz, z_recv.at[0])
    rows = xys * 32
    row = lax.broadcasted_iota(jnp.int32, (rows, tok), 0)
    side = (row // 16) % 2
    holder = (zh + side * (RUNS // 2)) % RUNS
    wanted = ((holder * xys + row // 32) * CAP + row % CAP).astype(F32)
    source = (row // CAP) % 4

    def build(q, _):
        for m in range(4):
            code = cz[4 * q + m][0:1, :].astype(F32)
            hit = jnp.where((wanted == code) & (source == m), 1.0, 0.0)
            place[q, :, m * tok : (m + 1) * tok] = hit.astype(BF16)
        return 0

    lax.fori_loop(0, quads, build, 0)

    def put(src, dst):
        def one(q, _):
            block = src[pl.ds(4 * q, 4)].reshape(4 * tok, src.shape[2])
            out = dot(place[q], block, ((1,), (0,))).astype(BF16)
            dst[:, :, pl.ds(pl.multiple_of(q * 16, 16), 16), :] = out.reshape(xys, 2, 16, src.shape[2])
            return 0

        lax.fori_loop(0, quads, one, 0)

    def take(src, dst):
        def one(q, _):
            block = src[:, :, pl.ds(pl.multiple_of(q * 16, 16), 16), :].reshape(rows, src.shape[3])
            out = dot(place[q], block, ((0,), (0,))).astype(BF16)
            dst[pl.ds(4 * q, 4)] = out.reshape(4, tok, src.shape[3])
            return 0

        lax.fori_loop(0, quads, one, 0)

    done(hz, z_recv.at[1])
    put(hz, hx)
    x_out(hx, hr, 0)
    done(gz, z_recv.at[2])
    weights = remote(w, w2, p_send.at[0], p_recv.at[0], partner)
    weights.start()
    put(gz, gx)
    x_out(gx, gr, 1)

    done(hr, x_recv.at[0])
    halves = remote(hr, hr2, b_send.at[0], b_recv.at[0], sibling)
    halves.start()
    done(gr, x_recv.at[1])
    halves.wait_recv()

    blocks = min(4, xys)
    per = xys // blocks
    slots = near * 2 * CAP
    mine_at = pl.multiple_of(c * half, half)
    other_at = pl.multiple_of(other * half, half)

    def chunk(ref, b, s):
        return ref[pl.ds(b * per, per), s].reshape(per * slots, ref.shape[3])

    def forward(wref, s):
        def one(b, _):
            out = dot(chunk(hr, b, s), wref[pl.ds(mine_at, half), :], ((1,), (0,)))
            out += dot(chunk(hr2, b, s), wref[pl.ds(other_at, half), :], ((1,), (0,)))
            ox[pl.ds(b * per, per), s] = out.astype(BF16).reshape(per, slots, cols)
            return 0

        lax.fori_loop(0, blocks, one, 0)

    def backward(wref, s):
        def one(b, _):
            g = chunk(gr, b, s)
            keep = dot(g, wref[pl.ds(mine_at, half), :], ((1,), (1,))).astype(BF16)
            give = dot(g, wref[pl.ds(other_at, half), :], ((1,), (1,))).astype(BF16)
            pk[pl.ds(b * per, per), s] = keep.reshape(per, slots, half)
            ps[pl.ds(b * per, per), s] = give.reshape(per, slots, half)
            return 0

        lax.fori_loop(0, blocks, one, 0)

    part = min(256, half)
    swapped = flag[0:1, 0:1] > 0.5

    def outer(ref, start):
        def one(i, _):
            at = pl.multiple_of(i * part, part)
            sums = []
            for s in range(2):
                lhs = ref[:, s, :, pl.ds(at, part)].reshape(xys * slots, part)
                sums.append(dot(lhs, gr[:, s].reshape(xys * slots, cols), ((0,), (0,))))
            to = pl.ds(pl.multiple_of(start + at, part), part)
            dsend[to, :] = jnp.where(swapped, sums[0], sums[1]).astype(BF16)
            dkeep[to, :] = jnp.where(swapped, sums[1], sums[0])
            return 0

        lax.fori_loop(0, half // part, one, 0)

    forward(w, 0)
    backward(w, 0)
    outer(hr, c * half)
    outer(hr2, other * half)
    grads = remote(dsend, drecv, p_send.at[1], p_recv.at[1], partner)
    grads.start()

    weights.wait_recv()
    backward(w2, 1)
    partial = remote(ps, pr, b_send.at[1], b_recv.at[1], sibling)
    partial.start()
    forward(w2, 1)
    x_out(ox, ot, 2)
    partial.wait_recv()

    def pair(b, _):
        at = pl.ds(b * per, per)
        px[at] = (pk[at].astype(F32) + pr[at].astype(F32)).astype(BF16)
        return 0

    lax.fori_loop(0, blocks, pair, 0)
    x_out(px, pt, 3)
    done(ot, x_recv.at[2])
    take(ot, ou)
    z_back(ou, oz, 3)
    done(pt, x_recv.at[3])
    take(pt, pu)
    z_back(pu, pz, 4)

    grads.wait_recv()
    wgrad[...] = (dkeep[...] + drecv[...].astype(F32)).astype(BF16)

    done(oz, z_recv.at[3])
    total = jnp.zeros((tok, 1), F32)
    for k in range(low):
        first = (k + low - 1) * 2
        second = (near - 1) * 2 if k == 0 else (k - 1) * 2
        for core in range(2):
            value = oz[first + core].astype(F32) + oz[second + core].astype(F32)
            at = pl.ds(pl.multiple_of((((zl + k) % low) * 2 + core) * cols, cols), cols)
            mixed[:, at] = (probs[...] * value).astype(BF16)
            total += jnp.sum(og[:, at].astype(F32) * value, axis=1, keepdims=True)
    pgrad[...] = total

    done(pz, z_recv.at[4])
    for core in range(2):
        value = pz[core].astype(F32)
        for k in range(1, near):
            value += pz[2 * k + core].astype(F32)
        hgrad[:, core * half : (core + 1) * half] = value.astype(BF16)

    for k, ref in enumerate((cz, hz, gz, oz, pz)):
        done(ref.at[pl.ds(0, 2 * near - 1)], z_send.at[k])
    for k, ref in enumerate((hr, gr, ot, pt)):
        done(ref.at[pl.ds(0, xys - 1)], x_send.at[k])
    halves.wait_send()
    partial.wait_send()
    weights.wait_send()
    grads.wait_send()


def shards(xys, low, hidden, probs, expert_ids, swap_plan, down_weight, out_grad):
    tok, _, width_ff = hidden.shape
    width = out_grad.shape[1]
    cols = down_weight.shape[2]
    half = width_ff // 2
    near = 2 * low
    slots = near * 2 * CAP
    mine = lax.axis_index("expert")
    ids = expert_ids[:, 0]
    order = jnp.arange(tok, dtype=jnp.int32)
    before = (ids[:, None] == ids[None, :]) & (order[:, None] < order[None, :])
    code = ids * CAP + jnp.sum(before.astype(jnp.int32), axis=0)
    codes = jnp.broadcast_to(code.astype(F32)[None, :], (16, tok)).astype(BF16)
    experts = swap_plan.shape[0]
    own = jnp.sum(jnp.where(jnp.arange(experts, dtype=jnp.int32) == mine, swap_plan, 0))
    flag = jnp.broadcast_to((own == 1).astype(F32), (8, 128))
    vm = pl.BlockSpec(memory_space=pltpu.VMEM)
    S = jax.ShapeDtypeStruct
    V = pltpu.VMEM
    plane_h, plane_g = (xys, 2, slots, half), (xys, 2, slots, cols)
    line_h, line_g = (2 * near, tok, half), (2 * near, tok, cols)
    dma = pltpu.SemaphoreType.DMA
    mixed, hgrad, pgrad, wgrad = pl.pallas_call(
        functools.partial(kernel, (xys, low, tok)),
        out_shape=(
            S((tok, width), BF16),
            S((tok, width_ff), BF16),
            S((tok, 1), F32),
            S((width_ff, cols), BF16),
        ),
        in_specs=[vm] * 6,
        out_specs=(vm,) * 4,
        scratch_shapes=[
            V((2, tok, half), BF16), V((2 * low, tok, cols), BF16),
            V(line_h, BF16), V(line_g, BF16), V((2 * near, 16, tok), BF16),
            V(plane_h, BF16), V(plane_g, BF16), V(plane_h, BF16), V(plane_h, BF16), V(plane_g, BF16),
            V((near // 2, xys * 32, 4 * tok), BF16), V((width_ff, cols), BF16),
            V(plane_g, BF16), V(plane_g, BF16), V(line_g, BF16), V(line_g, BF16),
            V(plane_h, BF16), V(plane_h, BF16), V(plane_h, BF16), V(plane_h, BF16), V(plane_h, BF16),
            V(line_h, BF16), V(line_h, BF16),
            V((width_ff, cols), BF16), V((width_ff, cols), F32), V((width_ff, cols), BF16),
            dma((5,)), dma((5,)), dma((4,)), dma((4,)), dma((2,)), dma((2,)), dma((2,)), dma((2,)),
        ],
        compiler_params=pltpu.CompilerParams(
            collective_id=0, has_side_effects=True, vmem_limit_bytes=60 << 20
        ),
    )(hidden[:, 0, :], out_grad, probs, codes, flag, down_weight[0])
    return mixed, hgrad[:, None, :], pgrad, wgrad[None]


def solution(mesh):
    experts, groups = mesh.shape["expert"], mesh.shape["dp"]
    tokens, line = P(("expert", "dp"), None), P(("expert", "dp"), None, None)
    weights = P("expert", None, "dp")
    return jax.shard_map(
        functools.partial(shards, experts // RUNS, groups // 2),
        mesh=mesh,
        in_specs=(line, tokens, tokens, P(), weights, tokens),
        out_specs=(tokens, line, tokens, weights),
        check_vma=False,
    )
```

time: 580 us -> 409 us (0.71); the launches traced: 569 us -> 409 us
  Pallas kernels: 0 us -> 398 us
  waiting for transfers between devices: 387 us -> 0 us
  starting transfers between devices: 118 us -> 0 us
  matrix products: 22.9 us -> 0 us
  local copies, waits for them, and re-layouts: 22.6 us -> 8.79 us
  between operations: 14.8 us -> 1.32 us
    pallas_call x0 -> x1, Pallas kernels: none -> 398 us  [shards(): pl.pallas_call(functools.partial(kernel, (xys, low, tok)), out_shape=(S((...]
    all_to_all x6 -> x0, waiting for transfers between devices: 261 us -> none  [the longest x1 94 us: shards(): lax.all_to_all(regrouped.reshape(experts, capacity, groups * cols), 'expe...]
    ppermute x1 -> x0, waiting for transfers between devices: 126 us -> none  [partner(): lax.ppermute(value, axis, [(i, i ^ 1 << apart) for i in range(lax.axis_si...]
    all_to_all x6 -> x0, starting transfers between devices: 112 us -> none  [the longest x1 47.5 us: shards(): lax.all_to_all(lax.all_to_all(grad_send, 'expert', split_axis=0, concat_a...]
    dot_general x7 -> x0, matrix products: 22.9 us -> none  [the longest x1 6.22 us: shards(): lax.dot_general(grad_all, weights, (((1,), (1,)), ((), ())), preferred_el...]
    reshape x8 -> x0, local copies, waits for them, and re-layouts: 16 us -> none  [the longest x1 2.79 us: shards(): regrouped.reshape(experts, capacity, groups * cols)]
    ppermute x1 -> x0, starting transfers between devices: 6.11 us -> none  [partner(): lax.ppermute(value, axis, [(i, i ^ 1 << apart) for i in range(lax.axis_si...]
    unnamed x11 -> x15, local copies, waits for them, and re-layouts: 1.71 us -> 7.6 us
  transfers between devices with their start and end apart: 9 -> 0, of which waited for: 7 -> 0; matrix products, arithmetic and copies ran while one was open for 7% -> 0% of each run, Pallas kernels for 0% -> 0%
where the time goes in v1:
time: 409 us
  Pallas kernels  398 us (97%)
  local copies, waits for them, and re-layouts  8.79 us (2%)
    pallas_call x1, Pallas kernels, shards(): pl.pallas_call(functools.partial(kernel, (xys, low, tok)), out_shape=(S((...  398 us

profile of v1, /device:TPU:25, one launch (start us, length us, event | category | flops | bytes accessed | tf_op | source)
XLA Modules:
  0.0 408.6 jit_solution(7552479889653675733)
XLA Ops:
  0.6 0.0 copy-start.3
  0.6 0.6 copy-done.3
  1.3 0.6 fusion.1
  2.6 0.0 copy-start.4
  2.6 0.6 copy-done.4
  3.2 0.1 convert_reduce_fusion
  3.3 0.6 broadcast_in_dim.21.codes
  3.9 0.0 copy-start.2
  3.9 0.6 broadcast_in_dim.23.flag
  4.5 0.1 copy-done.2
  4.6 0.7 copy.12.probs
  5.3 397.7 %shard_map.93 = (bf16[128,4096]{1,0:T(8,128)(2,1)}, bf16[128,1024]{1,0:T(8,128)(2,1)}, f32[128,1]{1,0:T(8,128)}, bf16[1024,512]{1,0:T(8,128)(2,1)}) custom-call(bf16[128,1024]{1,0:T(8,128)(2,1)} %bitcast.8, bf16[128,4096]{1,0:T(8,128)(2,1)} %og.1, f32[128,1]{1,0:T(8,128)} %copy.12.probs, bf16[16,128]{1,0:T(8,128)(2,1)} %broadcast_in_dim.21.codes, ...), custom_call_target="tpu_custom_call" | custom-call | tf_op jit(solution)/shard_map/pallas_call | solution.py:317
  403.1 1.4 copy.13
  404.5 0.0 copy-start.1
  404.5 0.0 copy-start
  404.5 2.4 copy.17
  406.9 0.0 copy-done.1
  406.9 0.7 copy.18
  407.6 0.0 copy-done
  407.6 1.0 copy.19
  (1 shorter events, 0.0 us)
Async XLA Ops:
  0.6 0.7 copy-start.3
  2.6 0.7 copy-start.4
  3.9 0.7 copy-start.2
  404.5 2.4 copy-start.1
  404.5 3.1 copy-start

commit v2 on v1

v2 whole, which is shorter than its diff:
```python
import functools

import jax
import jax.numpy as jnp
from jax import lax
from jax.experimental import pallas as pl
from jax.experimental.pallas import tpu as pltpu
from jax.sharding import PartitionSpec as P

MESH = pl.DeviceIdType.MESH
RUNS = 4
CAP = 4
BF16, F32 = jnp.bfloat16, jnp.float32


def dot(a, b, dims):
    return lax.dot_general(a, b, (dims, ((), ())), preferred_element_type=F32)


def done(view, sem):
    pltpu.make_async_copy(view, view, sem).wait()


def kernel(
    sizes, hid, og, probs, codes, flag, w, mixed, hgrad, pgrad, wgrad,
    hs, hs2, gs, hz, gz, cz, xs, xr, hr2, place, w2, rs, rt, ou, oz,
    ps, pk, pr, pu, pz, dsend, dkeep, drecv,
    c_send, c_recv, g_send, g_recv, o_send, o_recv, x_send, x_recv, y_send, y_recv,
    b_send, b_recv, s_send, s_recv, t_send, t_recv, p_send, p_recv, h_send, h_recv, f_send, f_recv,
):
    xys, low, tok = sizes
    chips = RUNS * low
    near = 2 * low
    half = hid.shape[1] // 2
    cols = w.shape[1]
    quads = near // 2
    e, d = lax.axis_index("expert"), lax.axis_index("dp")
    zh, xy, zl, c = e // xys, e % xys, d // 2, d % 2
    z = zh * low + zl
    other = 1 - c

    def at_chip(step, core):
        to = (z + step + chips) % chips
        return (to // low) * xys + xy, (to % low) * 2 + core

    far = low * (1 - 2 * c)
    partner = ((zh + RUNS // 2) % RUNS * xys + xy, d)
    sibling = (e, zl * 2 + other)

    def in_plane(n):
        to = (xy + n) % xys
        return to, (zh * xys + to, d)

    def remote(src, dst, ssem, rsem, to):
        return pltpu.make_async_remote_copy(
            src_ref=src, dst_ref=dst, send_sem=ssem, recv_sem=rsem, device_id=to, device_id_type=MESH
        )

    barrier = pltpu.get_barrier_semaphore()

    def greet(to):
        pl.semaphore_signal(barrier, inc=1, device_id=to, device_id_type=MESH)

    def step_of(i):
        return jnp.where(i < low - 1, i - (low - 1), i - (low - 2))

    def hello_z(i, _):
        for core in range(2):
            greet(at_chip(step_of(i), core))
        return 0

    def hello_xy(n, _):
        greet(in_plane(n)[1])
        return 0

    lax.fori_loop(0, near - 2, hello_z, 0)
    for core in range(2):
        greet(at_chip(low, core))
        greet(at_chip(-low, core))
    greet(sibling)
    greet(partner)
    lax.fori_loop(1, xys, hello_xy, 0)
    pl.semaphore_wait(barrier, 2 * (near - 2) + 4 + 2 + xys - 1)

    centre = (low - 1) * 2
    rows = xys * 32
    last_step = {slot: slot - low + 1 for slot in range(near - 1)}
    level = {**{slot: abs(step) for slot, step in last_step.items()}, near - 1: low}
    order = sorted(range(quads), key=lambda q: max(level[2 * q], level[2 * q + 1]))
    mine_at = pl.multiple_of(c * half, half)
    other_at = pl.multiple_of(other * half, half)
    right, left = pl.ds(half, cols), pl.ds(0, half)

    def band(q):
        return pl.ds(q * 16, 16)

    def in_quad(q, ref):
        return ref.at[pl.ds(4 * q, 4)]

    def z_out(src_of, dst, ssem, rsem, levels):
        def one(step, slot, core):
            remote(src_of(step, core), dst.at[slot * 2 + c], ssem, rsem(slot // 2), at_chip(step, core)).start()

        for k in levels:
            if k == 0:
                pltpu.make_async_copy(src_of(0, c), dst.at[centre + c], rsem((low - 1) // 2)).start()
                remote(src_of(0, other), dst.at[centre + c], ssem, rsem((low - 1) // 2), sibling).start()
            elif k < low:
                for step in (k, -k):
                    for core in range(2):
                        one(step, low - 1 - step, core)
            else:
                for core in range(2):
                    one(far, near - 1, core)

    def z_back(q):
        def one(step, slot, core, to):
            remote(ou.at[slot * 2 + core], oz.at[(low - 1 - step) * 2 + c], o_send, o_recv, to).start()

        for slot in (2 * q, 2 * q + 1):
            if slot == near - 1:
                for core in range(2):
                    remote(
                        ou.at[slot * 2 + core], oz.at[slot * 2 + c], o_send, o_recv,
                        at_chip(low * (2 * core - 1), core),
                    ).start()
            elif slot == low - 1:
                one(0, slot, other, sibling)
                pltpu.make_async_copy(ou.at[slot * 2 + c], oz.at[slot * 2 + c], o_recv).start()
            else:
                for core in range(2):
                    one(last_step[slot], slot, core, at_chip(last_step[slot], core))

    def x_out(src, dst, q, ssem, rsem):
        def go(n, _):
            to, dev = in_plane(n)
            remote(src.at[to, :, band(q)], dst.at[xy, :, band(q)], ssem, rsem, dev).start()
            return 0

        lax.fori_loop(1, xys, go, 0)
        pltpu.make_async_copy(src.at[xy, :, band(q)], dst.at[xy, :, band(q)], rsem).start()

    hs[...] = hid[:, pl.ds(other_at, half)]
    mates = remote(hs, hz.at[centre + c], b_send.at[0], b_recv.at[0], sibling)
    mates.start()
    hz[centre + c] = hid[:, pl.ds(mine_at, half)]

    def hop(way, k):
        if k == low:
            src, dst = (hz.at[0], hz.at[2 * near - 2]) if way > 0 else (hz.at[2 * near - 3], hz.at[2 * near - 1])
        else:
            src, dst = (centre - 2 * way * (k - 1)), (centre - 2 * way * k)
            src, dst = hz.at[pl.ds(src, 2)], hz.at[pl.ds(dst, 2)]
        n = 0 if way > 0 else 1
        return remote(src, dst, h_send.at[n, k - 1], h_recv.at[n, k - 1], at_chip(way, c))

    z_out(lambda step, core: codes, cz, c_send, lambda q: c_recv, range(low + 1))
    mates.wait_recv()
    for way in (1, -1):
        hop(way, 1).start()
    for g in range(gs.shape[0]):
        up = og[:, g * cols : (g + 1) * cols].astype(F32)
        gs[g] = (probs[...] * up).astype(BF16)

    def g_out(*levels):
        z_out(
            lambda step, core: gs.at[((zl + step + low) % low) * 2 + core], gz, g_send, lambda q: g_recv.at[q], levels
        )

    g_out(0, 1)

    done(cz, c_recv)
    row = lax.broadcasted_iota(jnp.int32, (rows, tok), 0)
    side = (row // 16) % 2
    holder = (zh + side * (RUNS // 2)) % RUNS
    wanted = ((holder * xys + row // 32) * CAP + row % CAP).astype(F32)
    source = (row // CAP) % 4

    def build(q, _):
        for m in range(4):
            code = cz[4 * q + m][0:1, :].astype(F32)
            hit = jnp.where((wanted == code) & (source == m), 1.0, 0.0)
            place[q, :, m * tok : (m + 1) * tok] = hit.astype(BF16)
        return 0

    lax.fori_loop(0, quads, build, 0)

    def put(src, q, at):
        block = src[pl.ds(4 * q, 4)].reshape(4 * tok, src.shape[2])
        out = dot(place[q], block, ((1,), (0,))).astype(BF16)
        xs[:, :, band(q), at] = out.reshape(xys, 2, 16, src.shape[2])

    def take(q, at, dst):
        block = rt[:, :, band(q), at].reshape(rows, dst.shape[2])
        out = dot(place[q], block, ((0,), (0,))).astype(BF16)
        dst[pl.ds(4 * q, 4)] = out.reshape(4, tok, dst.shape[2])

    def halves(q):
        return remote(
            xr.at[:, :, band(q), left], hr2.at[:, :, band(q)], s_send.at[q], s_recv.at[q], sibling
        )

    def chunk(ref, q, s, at):
        return ref[:, s, band(q), at].reshape(xys * 16, half)

    def forward(wref, q, s):
        out = dot(chunk(xr, q, s, left), wref[pl.ds(mine_at, half), :], ((1,), (0,)))
        out += dot(chunk(hr2, q, s, left), wref[pl.ds(other_at, half), :], ((1,), (0,)))
        rs[:, s, band(q), left] = out.astype(BF16).reshape(xys, 16, cols)

    def backward(wref, q, s):
        g = chunk(xr, q, s, right)
        keep = dot(g, wref[pl.ds(mine_at, half), :], ((1,), (1,))).astype(BF16)
        give = dot(g, wref[pl.ds(other_at, half), :], ((1,), (1,))).astype(BF16)
        pk[:, s, band(q)] = keep.reshape(xys, 16, half)
        ps[:, s, band(q)] = give.reshape(xys, 16, half)

    def arrive(q):
        done(xr.at[:, :, band(q)], x_recv.at[q])
        halves(q).start()

    def own(q):
        backward(w, q, 0)
        halves(q).wait_recv()
        forward(w, q, 0)

    weights = remote(w, w2, p_send.at[0], p_recv.at[0], partner)
    for n, q in enumerate(order):
        for way in (1, -1):
            hop(way, n + 1).wait_recv()
        if n + 1 < low:
            for way in (1, -1):
                hop(way, n + 2).start()
            g_out(n + 2)
        if n == max(low - 2, 0):
            weights.start()
        put(hz, q, left)
        done(in_quad(q, gz), g_recv.at[q])
        put(gz, q, right)
        x_out(xs, xr, q, x_send.at[q], x_recv.at[q])
        if n > 0:
            arrive(order[n - 1])
        if n > 1:
            own(order[n - 2])
    arrive(order[-1])
    for q in order[-2:]:
        own(q)

    slots = near * 2 * CAP
    part = min(256, half)
    swapped = flag[0:1, 0:1] > 0.5

    def outer(ref, start):
        def one(i, _):
            at = pl.multiple_of(i * part, part)
            sums = []
            for s in range(2):
                lhs = ref[:, s, :, pl.ds(at, part)].reshape(xys * slots, part)
                sums.append(dot(lhs, xr[:, s, :, right].reshape(xys * slots, cols), ((0,), (0,))))
            to = pl.ds(pl.multiple_of(start + at, part), part)
            dsend[to, :] = jnp.where(swapped, sums[0], sums[1]).astype(BF16)
            dkeep[to, :] = jnp.where(swapped, sums[1], sums[0])
            return 0

        lax.fori_loop(0, half // part, one, 0)

    outer(xr, c * half)
    outer(hr2, other * half)
    grads = remote(dsend, drecv, p_send.at[1], p_recv.at[1], partner)

    def partial(q):
        return remote(ps.at[:, :, band(q)], pr.at[:, :, band(q)], t_send.at[q], t_recv.at[q], sibling)

    def pair(q):
        partial(q).wait_recv()
        value = pk[:, :, band(q)].astype(F32) + pr[:, :, band(q)].astype(F32)
        rs[:, :, band(q), right] = value.astype(BF16)
        x_out(rs, rt, q, y_send.at[q], y_recv.at[q])

    weights.wait_recv()
    grads.start()
    back = order[::-1]
    for n, q in enumerate(back):
        backward(w2, q, 1)
        partial(q).start()
        forward(w2, q, 1)
        if n > 0:
            pair(back[n - 1])
    pair(back[-1])

    def fold(way, k):
        n = 0 if way > 0 else 1
        if k == low:
            src = pu.at[pl.ds(2 * near - 1, 1)] if way > 0 else pu.at[pl.ds(2 * near - 2, 1)]
            dst = pz.at[n, 0, pl.ds(0, 1)]
        else:
            src, dst = pu.at[pl.ds(centre + 2 * way * k, 2)], pz.at[n, low - k]
        return remote(src, dst, f_send.at[n, k - 1], f_recv.at[n, k - 1], at_chip(way, c))

    def add(way, k):
        n = 0 if way > 0 else 1
        fold(way, k + 1).wait_recv()
        if k + 1 == low:
            at = centre + 2 * way * k + 1 - n
            pu[at] = (pu[at].astype(F32) + pz[n, 0, 0].astype(F32)).astype(BF16)
        else:
            at = pl.ds(centre + 2 * way * k, 2)
            pu[at] = (pu[at].astype(F32) + pz[n, low - k - 1].astype(F32)).astype(BF16)

    for n, q in enumerate(back):
        done(rt.at[:, :, band(q)], y_recv.at[q])
        take(q, right, pu)
        for way in (1, -1):
            if n > 0:
                add(way, low - n)
            fold(way, low - n).start()
        take(q, left, ou)
        z_back(q)
    for way in (1, -1):
        add(way, 0)
    last = remote(pu.at[centre + other], hs2, b_send.at[1], b_recv.at[1], sibling)
    last.start()
    hgrad[:, pl.ds(mine_at, half)] = pu[centre + c]

    grads.wait_recv()
    wgrad[...] = (dkeep[...] + drecv[...].astype(F32)).astype(BF16)

    done(oz, o_recv)
    total = jnp.zeros((tok, 1), F32)
    for k in range(low):
        first = (k + low - 1) * 2
        second = (near - 1) * 2 if k == 0 else (k - 1) * 2
        for core in range(2):
            value = oz[first + core].astype(F32) + oz[second + core].astype(F32)
            at = pl.ds(pl.multiple_of((((zl + k) % low) * 2 + core) * cols, cols), cols)
            mixed[:, at] = (probs[...] * value).astype(BF16)
            total += jnp.sum(og[:, at].astype(F32) * value, axis=1, keepdims=True)
    pgrad[...] = total
    last.wait_recv()
    hgrad[:, pl.ds(other_at, half)] = hs2[...]

    for ref, sem in ((cz, c_send), (gz, g_send), (oz, o_send)):
        done(ref.at[pl.ds(0, 2 * near - 1)], sem)
    for way in (1, -1):
        for k in range(1, low + 1):
            hop(way, k).wait_send()
            fold(way, k).wait_send()
    for q in range(quads):
        done(xr.at[pl.ds(0, xys - 1), :, band(q)], x_send.at[q])
        done(rt.at[pl.ds(0, xys - 1), :, band(q)], y_send.at[q])
        halves(q).wait_send()
        partial(q).wait_send()
    mates.wait_send()
    last.wait_send()
    weights.wait_send()
    grads.wait_send()


def shards(xys, low, hidden, probs, expert_ids, swap_plan, down_weight, out_grad):
    tok, _, width_ff = hidden.shape
    width = out_grad.shape[1]
    cols = down_weight.shape[2]
    half = width_ff // 2
    near = 2 * low
    slots = near * 2 * CAP
    mine = lax.axis_index("expert")
    ids = expert_ids[:, 0]
    order = jnp.arange(tok, dtype=jnp.int32)
    before = (ids[:, None] == ids[None, :]) & (order[:, None] < order[None, :])
    code = ids * CAP + jnp.sum(before.astype(jnp.int32), axis=0)
    codes = jnp.broadcast_to(code.astype(F32)[None, :], (16, tok)).astype(BF16)
    experts = swap_plan.shape[0]
    own = jnp.sum(jnp.where(jnp.arange(experts, dtype=jnp.int32) == mine, swap_plan, 0))
    flag = jnp.broadcast_to((own == 1).astype(F32), (8, 128))
    vm = pl.BlockSpec(memory_space=pltpu.VMEM)
    S = jax.ShapeDtypeStruct
    V = pltpu.VMEM
    plane, wide = (xys, 2, slots, half), (xys, 2, slots, half + cols)
    line_h, line_g = (2 * near, tok, half), (2 * near, tok, cols)
    dma = pltpu.SemaphoreType.DMA
    quads = near // 2
    mixed, hgrad, pgrad, wgrad = pl.pallas_call(
        functools.partial(kernel, (xys, low, tok)),
        out_shape=(
            S((tok, width), BF16),
            S((tok, width_ff), BF16),
            S((tok, 1), F32),
            S((width_ff, cols), BF16),
        ),
        in_specs=[vm] * 6,
        out_specs=(vm,) * 4,
        scratch_shapes=[
            V((tok, half), BF16), V((tok, half), BF16), V((2 * low, tok, cols), BF16),
            V(line_h, BF16), V(line_g, BF16), V((2 * near, 16, tok), BF16),
            V(wide, BF16), V(wide, BF16), V(plane, BF16),
            V((quads, xys * 32, 4 * tok), BF16), V((width_ff, cols), BF16),
            V(wide, BF16), V(wide, BF16), V(line_g, BF16), V(line_g, BF16),
            V(plane, BF16), V(plane, BF16), V(plane, BF16),
            V(line_h, BF16), V((2, low, 2, tok, half), BF16),
            V((width_ff, cols), BF16), V((width_ff, cols), F32), V((width_ff, cols), BF16),
            dma, dma, dma, dma((quads,)), dma, dma,
            dma((quads,)), dma((quads,)), dma((quads,)), dma((quads,)), dma((2,)), dma((2,)),
            dma((quads,)), dma((quads,)), dma((quads,)), dma((quads,)), dma((2,)), dma((2,)),
            dma((2, low)), dma((2, low)), dma((2, low)), dma((2, low)),
        ],
        compiler_params=pltpu.CompilerParams(
            collective_id=0, has_side_effects=True, vmem_limit_bytes=60 << 20
        ),
    )(hidden[:, 0, :], out_grad, probs, codes, flag, down_weight[0])
    return mixed, hgrad[:, None, :], pgrad, wgrad[None]


def solution(mesh):
    experts, groups = mesh.shape["expert"], mesh.shape["dp"]
    tokens, line = P(("expert", "dp"), None), P(("expert", "dp"), None, None)
    weights = P("expert", None, "dp")
    return jax.shard_map(
        functools.partial(shards, experts // RUNS, groups // 2),
        mesh=mesh,
        in_specs=(line, tokens, tokens, P(), weights, tokens),
        out_specs=(tokens, line, tokens, weights),
        check_vma=False,
    )
```

time: 409 us -> 346 us (0.85)
  Pallas kernels: 398 us -> 334 us
    pallas_call x1, Pallas kernels: 398 us -> 334 us  [shards(): pl.pallas_call(functools.partial(kernel, (xys, low, tok)), out_shape=(S((...]
where the time goes in v2:
time: 346 us; the launch traced here: 345 us
  Pallas kernels  334 us (97%)
  local copies, waits for them, and re-layouts  8.79 us (3%)
    pallas_call x1, Pallas kernels, shards(): pl.pallas_call(functools.partial(kernel, (xys, low, tok)), out_shape=(S((...  334 us
    unnamed x15, local copies, waits for them, and re-layouts  7.6 us

profile of v2, /device:TPU:25, one launch (start us, length us, event | category | flops | bytes accessed | tf_op | source)
XLA Modules:
  0.0 344.9 jit_solution(15425517021747579091)
XLA Ops:
  0.6 0.0 copy-start.3
  0.6 0.6 copy-done.3
  1.3 0.6 fusion.1
  2.6 0.0 copy-start.4
  2.6 0.6 copy-done.4
  3.2 0.1 convert_reduce_fusion
  3.3 0.6 broadcast_in_dim.21.codes
  3.9 0.0 copy-start.2
  3.9 0.6 broadcast_in_dim.23.flag
  4.5 0.1 copy-done.2
  4.6 0.7 copy.12.probs
  5.3 334.1 %shard_map.93 = (bf16[128,4096]{1,0:T(8,128)(2,1)}, bf16[128,1024]{1,0:T(8,128)(2,1)}, f32[128,1]{1,0:T(8,128)}, bf16[1024,512]{1,0:T(8,128)(2,1)}) custom-call(bf16[128,1024]{1,0:T(8,128)(2,1)} %bitcast.8, bf16[128,4096]{1,0:T(8,128)(2,1)} %og.1, f32[128,1]{1,0:T(8,128)} %copy.12.probs, bf16[16,128]{1,0:T(8,128)(2,1)} %broadcast_in_dim.21.codes, ...), custom_call_target="tpu_custom_call" | custom-call | tf_op jit(solution)/shard_map/pallas_call | solution.py:382
  339.4 1.4 copy.13
  340.9 0.0 copy-start.1
  340.9 0.0 copy-start
  340.9 2.4 copy.17
  343.3 0.0 copy-done.1
  343.3 0.7 copy.18
  344.0 0.0 copy-done
  344.0 1.0 copy.19
  (1 shorter events, 0.0 us)
Async XLA Ops:
  0.6 0.7 copy-start.3
  2.6 0.7 copy-start.4
  3.9 0.7 copy-start.2
  340.9 2.4 copy-start.1
  340.9 3.1 copy-start

commit v3 on v2

--- a/solution.py
+++ b/solution.py
@@ -22,7 +22,8 @@
 
 
 def kernel(
-    sizes, hid, og, probs, codes, flag, w, mixed, hgrad, pgrad, wgrad,
+    sizes, hid, og, weight_row, ids, plan, w, mixed, hgrad, pgrad, wgrad,
+    codes, probs,
     hs, hs2, gs, hz, gz, cz, xs, xr, hr2, place, w2, rs, rt, ou, oz,
     ps, pk, pr, pu, pz, dsend, dkeep, drecv,
     c_send, c_recv, g_send, g_recv, o_send, o_recv, x_send, x_recv, y_send, y_recv,
@@ -80,7 +81,6 @@
     greet(sibling)
     greet(partner)
     lax.fori_loop(1, xys, hello_xy, 0)
-    pl.semaphore_wait(barrier, 2 * (near - 2) + 4 + 2 + xys - 1)
 
     centre = (low - 1) * 2
     rows = xys * 32
@@ -141,9 +141,15 @@
         pltpu.make_async_copy(src.at[xy, :, band(q)], dst.at[xy, :, band(q)], rsem).start()
 
     hs[...] = hid[:, pl.ds(other_at, half)]
+    hz[centre + c] = hid[:, pl.ds(mine_at, half)]
+    named = jnp.broadcast_to(ids[...].astype(F32), (tok, tok))
+    earlier = lax.broadcasted_iota(jnp.int32, (tok, tok), 0) < lax.broadcasted_iota(jnp.int32, (tok, tok), 1)
+    rank = jnp.sum(jnp.where((named == named.T) & earlier, 1.0, 0.0), axis=0, keepdims=True)
+    codes[...] = jnp.broadcast_to(ids[...].astype(F32) * CAP + rank, codes.shape).astype(BF16)
+    probs[...] = jnp.broadcast_to(weight_row[...], (tok, tok)).T[:, 0:1]
+    pl.semaphore_wait(barrier, 2 * (near - 2) + 4 + 2 + xys - 1)
     mates = remote(hs, hz.at[centre + c], b_send.at[0], b_recv.at[0], sibling)
     mates.start()
-    hz[centre + c] = hid[:, pl.ds(mine_at, half)]
 
     def hop(way, k):
         if k == low:
@@ -248,7 +254,8 @@
 
     slots = near * 2 * CAP
     part = min(256, half)
-    swapped = flag[0:1, 0:1] > 0.5
+    held = lax.broadcasted_iota(jnp.int32, plan.shape, 1) == e
+    swapped = jnp.sum(jnp.where(held, plan[...].astype(F32), 0.0), axis=1, keepdims=True) == 1.0
 
     def outer(ref, start):
         def one(i, _):
@@ -335,7 +342,7 @@
             at = pl.ds(pl.multiple_of((((zl + k) % low) * 2 + core) * cols, cols), cols)
             mixed[:, at] = (probs[...] * value).astype(BF16)
             total += jnp.sum(og[:, at].astype(F32) * value, axis=1, keepdims=True)
-    pgrad[...] = total
+    pgrad[...] = jnp.broadcast_to(total, (tok, tok)).T[0:1, :]
     last.wait_recv()
     hgrad[:, pl.ds(other_at, half)] = hs2[...]
 
@@ -363,15 +370,6 @@
     half = width_ff // 2
     near = 2 * low
     slots = near * 2 * CAP
-    mine = lax.axis_index("expert")
-    ids = expert_ids[:, 0]
-    order = jnp.arange(tok, dtype=jnp.int32)
-    before = (ids[:, None] == ids[None, :]) & (order[:, None] < order[None, :])
-    code = ids * CAP + jnp.sum(before.astype(jnp.int32), axis=0)
-    codes = jnp.broadcast_to(code.astype(F32)[None, :], (16, tok)).astype(BF16)
-    experts = swap_plan.shape[0]
-    own = jnp.sum(jnp.where(jnp.arange(experts, dtype=jnp.int32) == mine, swap_plan, 0))
-    flag = jnp.broadcast_to((own == 1).astype(F32), (8, 128))
     vm = pl.BlockSpec(memory_space=pltpu.VMEM)
     S = jax.ShapeDtypeStruct
     V = pltpu.VMEM
@@ -384,12 +382,13 @@
         out_shape=(
             S((tok, width), BF16),
             S((tok, width_ff), BF16),
-            S((tok, 1), F32),
+            S((1, tok), F32),
             S((width_ff, cols), BF16),
         ),
         in_specs=[vm] * 6,
         out_specs=(vm,) * 4,
         scratch_shapes=[
+            V((16, tok), BF16), V((tok, 1), F32),
             V((tok, half), BF16), V((tok, half), BF16), V((2 * low, tok, cols), BF16),
             V(line_h, BF16), V(line_g, BF16), V((2 * near, 16, tok), BF16),
             V(wide, BF16), V(wide, BF16), V(plane, BF16),
@@ -406,8 +405,8 @@
         compiler_params=pltpu.CompilerParams(
             collective_id=0, has_side_effects=True, vmem_limit_bytes=60 << 20
         ),
-    )(hidden[:, 0, :], out_grad, probs, codes, flag, down_weight[0])
-    return mixed, hgrad[:, None, :], pgrad, wgrad[None]
+    )(hidden[:, 0, :], out_grad, probs.reshape(1, tok), expert_ids.reshape(1, tok), swap_plan.reshape(1, -1), down_weight[0])
+    return mixed, hgrad[:, None, :], pgrad.reshape(tok, 1), wgrad[None]
 
 
 def solution(mesh):

time: 346 us -> 340 us (0.983)
  local copies, waits for them, and re-layouts: 8.79 us -> 4.58 us
    unnamed x15 -> x10, local copies, waits for them, and re-layouts: 7.6 us -> 4.58 us
where the time goes in v3:
time: 340 us; the launch traced here: 339 us
  Pallas kernels  334 us (98%)
  local copies, waits for them, and re-layouts  4.58 us (1%)
    pallas_call x1, Pallas kernels, shards(): pl.pallas_call(functools.partial(kernel, (xys, low, tok)), out_shape=(S((...  334 us

profile of v3, /device:TPU:25, one launch (start us, length us, event | category | flops | bytes accessed | tf_op | source)
XLA Modules:
  0.0 339.2 jit_solution(17051746706397421729)
XLA Ops:
  0.6 333.9 %shard_map.93 = (bf16[128,4096]{1,0:T(8,128)(2,1)}, bf16[128,1024]{1,0:T(8,128)(2,1)}, f32[1,128]{1,0:T(1,128)}, bf16[1024,512]{1,0:T(8,128)(2,1)}) custom-call(bf16[128,1024]{1,0:T(8,128)(2,1)} %bitcast.10, bf16[128,4096]{1,0:T(8,128)(2,1)} %og.1, f32[1,128]{1,0:T(1,128)} %bitcast.12, s32[1,128]{1,0:T(1,128)} %bitcast.13, s32[1,64]{1,0:T(1,128)} %bitcast.14, ...), custom_call_target="tpu_custom_call" | custom-call | tf_op jit(solution)/shard_map/pallas_call | solution.py:380
  334.6 0.0 copy-start.1
  334.6 0.0 copy-start
  334.6 2.4 copy.14
  337.0 0.0 copy-done.1
  337.0 0.0 copy-start.2
  337.0 0.7 copy.15
  337.7 0.0 copy-done.2
  337.7 0.5 copy.16
  338.2 0.0 copy-done
  338.2 1.0 copy.17
Async XLA Ops:
  334.6 2.4 copy-start.1
  334.6 3.6 %copy-start = (bf16[1024,512]{1,0:T(8,128)(2,1)S(1)}, bf16[1024,512]{1,0:T(8,128)(2,1)}, u32[]{:S(2)}) copy-start(bf16[1024,512]{1,0:T(8,128)(2,1)} %get-tuple-element.11) | copy-start | bytes 3145732
  337.0 0.7 copy-start.2

commit v4 on v3

--- a/solution.py
+++ b/solution.py
@@ -151,19 +151,22 @@
     mates = remote(hs, hz.at[centre + c], b_send.at[0], b_recv.at[0], sibling)
     mates.start()
 
-    def hop(way, k):
+    def hop(way, k, part):
+        lines = pl.ds(part * (tok // 2), tok // 2)
         if k == low:
-            src, dst = (hz.at[0], hz.at[2 * near - 2]) if way > 0 else (hz.at[2 * near - 3], hz.at[2 * near - 1])
+            src, dst = (0, 2 * near - 2) if way > 0 else (2 * near - 3, 2 * near - 1)
+            src, dst = hz.at[src, lines], hz.at[dst, lines]
         else:
             src, dst = (centre - 2 * way * (k - 1)), (centre - 2 * way * k)
-            src, dst = hz.at[pl.ds(src, 2)], hz.at[pl.ds(dst, 2)]
+            src, dst = hz.at[pl.ds(src, 2), lines], hz.at[pl.ds(dst, 2), lines]
         n = 0 if way > 0 else 1
-        return remote(src, dst, h_send.at[n, k - 1], h_recv.at[n, k - 1], at_chip(way, c))
+        return remote(src, dst, h_send.at[n, k - 1, part], h_recv.at[n, k - 1, part], at_chip(way, c))
 
     z_out(lambda step, core: codes, cz, c_send, lambda q: c_recv, range(low + 1))
     mates.wait_recv()
-    for way in (1, -1):
-        hop(way, 1).start()
+    for part in range(2):
+        for way in (1, -1):
+            hop(way, 1, part).start()
     for g in range(gs.shape[0]):
         up = og[:, g * cols : (g + 1) * cols].astype(F32)
         gs[g] = (probs[...] * up).astype(BF16)
@@ -232,11 +235,12 @@
 
     weights = remote(w, w2, p_send.at[0], p_recv.at[0], partner)
     for n, q in enumerate(order):
-        for way in (1, -1):
-            hop(way, n + 1).wait_recv()
+        for part in range(2):
+            for way in (1, -1):
+                hop(way, n + 1, part).wait_recv()
+                if n + 1 < low:
+                    hop(way, n + 2, part).start()
         if n + 1 < low:
-            for way in (1, -1):
-                hop(way, n + 2).start()
             g_out(n + 2)
         if n == max(low - 2, 0):
             weights.start()
@@ -350,7 +354,8 @@
         done(ref.at[pl.ds(0, 2 * near - 1)], sem)
     for way in (1, -1):
         for k in range(1, low + 1):
-            hop(way, k).wait_send()
+            for part in range(2):
+                hop(way, k, part).wait_send()
             fold(way, k).wait_send()
     for q in range(quads):
         done(xr.at[pl.ds(0, xys - 1), :, band(q)], x_send.at[q])
@@ -400,7 +405,7 @@
             dma, dma, dma, dma((quads,)), dma, dma,
             dma((quads,)), dma((quads,)), dma((quads,)), dma((quads,)), dma((2,)), dma((2,)),
             dma((quads,)), dma((quads,)), dma((quads,)), dma((quads,)), dma((2,)), dma((2,)),
-            dma((2, low)), dma((2, low)), dma((2, low)), dma((2, low)),
+            dma((2, low, 2)), dma((2, low, 2)), dma((2, low)), dma((2, low)),
         ],
         compiler_params=pltpu.CompilerParams(
             collective_id=0, has_side_effects=True, vmem_limit_bytes=60 << 20

time: 340 us -> 340 us (level)
  no operation moved by 1% of the time
where the time goes in v4:
time: 340 us; the launch traced here: 339 us
  Pallas kernels  334 us (98%)
  local copies, waits for them, and re-layouts  4.58 us (1%)
    pallas_call x1, Pallas kernels, shards(): pl.pallas_call(functools.partial(kernel, (xys, low, tok)), out_shape=(S((...  334 us

profile of v4, /device:TPU:25, one launch (start us, length us, event | category | flops | bytes accessed | tf_op | source)
XLA Modules:
  0.0 339.3 jit_solution(3810156806928470736)
XLA Ops:
  0.6 334.1 %shard_map.93 = (bf16[128,4096]{1,0:T(8,128)(2,1)}, bf16[128,1024]{1,0:T(8,128)(2,1)}, f32[1,128]{1,0:T(1,128)}, bf16[1024,512]{1,0:T(8,128)(2,1)}) custom-call(bf16[128,1024]{1,0:T(8,128)(2,1)} %bitcast.10, bf16[128,4096]{1,0:T(8,128)(2,1)} %og.1, f32[1,128]{1,0:T(1,128)} %bitcast.12, s32[1,128]{1,0:T(1,128)} %bitcast.13, s32[1,64]{1,0:T(1,128)} %bitcast.14, ...), custom_call_target="tpu_custom_call" | custom-call | tf_op jit(solution)/shard_map/pallas_call | solution.py:385
  334.7 0.0 copy-start.1
  334.7 0.0 copy-start
  334.8 2.4 copy.14
  337.1 0.0 copy-done.1
  337.1 0.0 copy-start.2
  337.1 0.7 copy.15
  337.9 0.0 copy-done.2
  337.9 0.5 copy.16
  338.4 0.0 copy-done
  338.4 1.0 copy.17
Async XLA Ops:
  334.7 2.4 copy-start.1
  334.7 3.6 %copy-start = (bf16[1024,512]{1,0:T(8,128)(2,1)S(1)}, bf16[1024,512]{1,0:T(8,128)(2,1)}, u32[]{:S(2)}) copy-start(bf16[1024,512]{1,0:T(8,128)(2,1)} %get-tuple-element.11) | copy-start | bytes 3145732
  337.1 0.7 copy-start.2
